TPU v7x, 512 devices: a whole 4x4x16 slice. The times are simulated.
512 devices in a mesh: row: 16 (over z), col: 32 (over y, x, core).
Axes of the slice: x: 4, y: 4, z: 16, core: 2. Of those that a mesh axis runs over, the one named last changes fastest.
Arguments:
- centroids: float32 [3, 32768], P(None, ('col', 'row')), may hold values from 0 to 1, as said below
- areas: float32 [32768], P(('col', 'row')), may hold values from 0.5 to 2
- conductance: float32 [32768], P(('col', 'row')), may hold values from 0.1 to 1
- power: float32 [16, 32768], P(None, ('col', 'row')), may hold values from -3 to 6
Outputs:
- solution: float32 [16, 32768], P(None, ('col', 'row'))
- residual: float32 [16, 32768], P(None, ('col', 'row'))
Inputs may be any that keep to these rules, and one draw needn't show every extreme that they name: `centroids`: panels lie on 16 parallel fins across the unit cube.
All inputs are finite; a program needn't handle non-finite values.
Results may differ from a plain program's by a relative error of at most 0.00039.
Values may be sent and summed in bfloat16 or wider, within the bound.
No kernel may reach another device: no remote copies, remote signals or barrier semaphores. Data moves between devices by JAX's collectives and lax.ppermute only.
A program may use at most 64 MiB of HBM per device.

v0:
```python
import math
import jax
import jax.numpy as jnp
from jax import lax
from jax.sharding import PartitionSpec as P


def kernel_tile(src, tgt, scale, delta2):
    dx = src[0][:, None] - tgt[0][None, :]
    dy = src[1][:, None] - tgt[1][None, :]
    dz = src[2][:, None] - tgt[2][None, :]
    dist2 = dx * dx + dy * dy + dz * dz
    return (src[3][:, None] * scale * lax.rsqrt(dist2 + delta2)).astype(jnp.bfloat16)


def inner(left, right):
    return jnp.dot(left, right.T, precision=lax.Precision.HIGHEST)


def lower_inverse(gram):
    factor = jnp.linalg.cholesky(gram)
    eye = jnp.eye(gram.shape[0], dtype=jnp.float32)
    return (factor, jax.scipy.linalg.solve_triangular(factor, eye, lower=True))


def reduce_small(terms):
    return lax.psum(terms, ("row", "col"))


def body(centroids, areas, conductance, power):
    high = lax.Precision.HIGHEST
    width = power.shape[1]
    nrhs = power.shape[0]
    panels = width * lax.axis_size("row") * lax.axis_size("col")
    scale = 4.0 / (math.pi * panels)
    delta2 = 16.0 / panels
    geom = jnp.concatenate([centroids, areas[None, :]], 0)
    sources = lax.all_gather(geom, "col", axis=1, tiled=True)
    targets = lax.all_gather(centroids, "row", axis=1, tiled=True)
    tgt_len = targets.shape[1]
    rhs, cond_row = (power, conductance[None, :])
    factor0, inverse0 = lower_inverse(reduce_small(inner(rhs, rhs)))
    basis = [jnp.dot(inverse0, rhs, precision=high)]
    blocks = {}
    for step in range(2):
        field = basis[step]
        empty = jnp.zeros((nrhs, tgt_len), jnp.float32)
        piece = lax.all_gather(field.astype(jnp.bfloat16), "col", axis=1, tiled=True)
        cols = piece.shape[1]
        step_len = width * max(1, 512 // width)
        turns = cols // step_len

        def one(turn, acc):
            vec = lax.dynamic_slice_in_dim(piece, turn * step_len, step_len, 1)
            src = lax.dynamic_slice_in_dim(sources, turn * step_len, step_len, 1)
            tile = kernel_tile(src, targets, scale, delta2)
            return acc + jnp.dot(vec, tile, preferred_element_type=jnp.float32)

        apply_total = lax.fori_loop(0, turns, one, empty)
        product = lax.psum_scatter(apply_total, "row", scatter_dimension=1, tiled=True)
        image = cond_row * field + product
        coeffs = list(reduce_small(tuple((inner(vec, image) for vec in basis))))
        for idx in range(step + 1):
            image = image - jnp.dot(coeffs[idx].T, basis[idx], precision=high)
        gram = reduce_small(inner(image, image))
        for idx in range(step + 1):
            blocks[idx, step] = coeffs[idx]
        factor, inverse = lower_inverse(gram)
        blocks[step + 1, step] = factor.T
        basis.append(jnp.dot(inverse, image, precision=high))
    hbar = jnp.zeros((3 * nrhs, 2 * nrhs), jnp.float32)
    for key in blocks:
        hbar = hbar.at[
            key[0] * nrhs : (key[0] + 1) * nrhs, key[1] * nrhs : (key[1] + 1) * nrhs
        ].set(blocks[key])
    target = jnp.zeros((3 * nrhs, nrhs), jnp.float32).at[:nrhs].set(factor0.T)
    normal = jnp.dot(hbar.T, hbar, precision=high)
    chol = jnp.linalg.cholesky(normal)
    coeff_y = jax.scipy.linalg.cho_solve((chol, True), jnp.dot(hbar.T, target, precision=high))
    coeff_z = target - jnp.dot(hbar, coeff_y, precision=high)
    solution = jnp.dot(coeff_y[:nrhs].T, basis[0], precision=high) + jnp.dot(
        coeff_y[nrhs:].T, basis[1], precision=high
    )
    residual = jnp.dot(coeff_z[:nrhs].T, basis[0], precision=high) + jnp.dot(
        coeff_z[nrhs : 2 * nrhs].T, basis[1], precision=high
    )
    residual = residual + jnp.dot(coeff_z[2 * nrhs :].T, basis[2], precision=high)
    return (solution, residual)


def solution(mesh):
    return jax.shard_map(
        body,
        mesh=mesh,
        in_specs=(
            P(None, ("col", "row")),
            P(("col", "row")),
            P(("col", "row")),
            P(None, ("col", "row")),
        ),
        out_specs=(P(None, ("col", "row")), P(None, ("col", "row"))),
        check_vma=False,
    )
```

profile of v0, /device:TPU:1, one launch (start us, length us, event | category | flops | bytes accessed | tf_op | source)
XLA Modules:
  0.0 797.1 jit_solution(8880030113008817273)
XLA Ops:
  7.3 0.6 copy-done
  8.0 111.0 %psum.42 = f32[16,16]{0,1:T(8,128)S(1)} all-reduce(f32[16,16]{0,1:T(8,128)S(1)} %fusion.59), channel_id=1, replica_groups=mesh['row'=16,'col'=32] {'row','col'}, use_global_device_ids=true, to_apply=%region_0.0 | all-reduce | flops 256 | bytes 2048 | tf_op jit(solution)/shard_map/psum | solution.py:27
  119.1 1.5 cholesky.94
  120.6 0.6 compare_reduce_fusion.2
  121.3 0.6 fusion.49
  121.9 1.2 custom-call.20
  123.1 0.2 fusion.30
  123.5 22.9 %all-gather = bf16[32,64,16]{1,2,0:T(8,128)(2,1)S(1)} all-gather(bf16[1,64,16]{1,2,0:T(8,128)(2,1)S(1)} %convert_bitcast_fusion.1), channel_id=1, replica_groups=mesh['row'=16,'col'=32] {'col'}, dimensions={0}, use_global_device_ids=true | all-gather | bytes 67584 | tf_op jit(solution)/shard_map/all_gather | solution.py:48
  146.5 0.2 reshape.234
  146.7 23.6 %all-gather.1 = f32[32,64,4]{1,2,0:T(4,128)S(1)} all-gather(f32[1,64,4]{1,2,0:T(4,128)S(1)} %maximum_bitcast_fusion), channel_id=1, replica_groups=mesh['row'=16,'col'=32] {'col'}, dimensions={0}, use_global_device_ids=true | all-gather | bytes 33792 | tf_op jit(solution)/shard_map/all_gather | solution.py:38
  170.4 19.9 %all-gather.2 = f32[16,64,3]{1,2,0:T(4,128)S(1)} all-gather(f32[1,64,3]{1,2,0:T(4,128)S(1)} %bitcast.175), channel_id=1, replica_groups=mesh['row'=16,'col'=32] {'row'}, dimensions={0}, use_global_device_ids=true | all-gather | bytes 13056 | tf_op jit(solution)/shard_map/all_gather | solution.py:39
  190.4 4.5 while.34
  190.5 1.0 convolution_add_fusion.7
  191.6 1.0 convolution_add_fusion.7
  192.8 1.0 convolution_add_fusion.7
  193.9 1.0 convolution_add_fusion.7
  194.9 1.0 copy.57
  196.0 59.8 %reduce-scatter.7.cloned.1.call-done = f32[64,16]{1,0:T(8,128)} async-done(((f32[1024,16]{1,0:T(8,128)}), f32[64,16]{1,0:T(8,128)}) %reduce-scatter.7.cloned.1.call-update) | async-done | bytes 4112
  255.8 0.8 copy.58
  256.7 111.7 %psum.43 = f32[16,16]{1,0:T(8,128)S(1)} all-reduce(f32[16,16]{1,0:T(8,128)S(1)} %fusion.46), channel_id=1, replica_groups=mesh['row'=16,'col'=32] {'row','col'}, use_global_device_ids=true, to_apply=%region_6.0 | all-reduce | flops 256 | bytes 2048 | tf_op jit(solution)/shard_map/psum | solution.py:27
  368.4 0.2 convolution_subtract_fusion.3
  368.7 100.0 %psum.44 = f32[16,16]{0,1:T(8,128)S(1)} all-reduce(f32[16,16]{0,1:T(8,128)S(1)} %fusion.61), channel_id=1, replica_groups=mesh['row'=16,'col'=32] {'row','col'}, use_global_device_ids=true, to_apply=%region_7.0 | all-reduce | flops 256 | bytes 2048 | tf_op jit(solution)/shard_map/psum | solution.py:27
  468.8 1.5 cholesky.105
  470.3 0.6 compare_reduce_fusion.1
  470.9 0.6 select_bitcast_fusion.1
  471.6 1.2 custom-call.21
  472.8 0.2 fusion.28
  473.2 24.4 %all-gather.3 = bf16[32,64,16]{1,2,0:T(8,128)(2,1)S(1)} all-gather(bf16[1,64,16]{1,2,0:T(8,128)(2,1)S(1)} %convert_bitcast_fusion), channel_id=1, replica_groups=mesh['row'=16,'col'=32] {'col'}, dimensions={0}, use_global_device_ids=true | all-gather | bytes 67584 | tf_op jit(solution)/shard_map/all_gather | solution.py:48
  497.6 0.2 reshape.240
  497.7 4.5 while.35
  497.9 1.0 convolution_add_fusion.8
  499.0 1.0 convolution_add_fusion.8
  500.1 1.0 convolution_add_fusion.8
  501.2 1.0 convolution_add_fusion.8
  502.3 1.0 copy.59
  503.3 0.6 fusion.58
  503.9 0.7 and_reduce_fusion
  504.6 0.5 scatter.21
  505.2 51.2 %reduce-scatter.9.cloned.1.call-done = f32[64,16]{1,0:T(8,128)} async-done(((f32[1024,16]{1,0:T(8,128)}), f32[64,16]{1,0:T(8,128)}) %reduce-scatter.9.cloned.1.call-update) | async-done | bytes 4112
  556.4 0.8 copy.60
  557.5 111.9 %all-reduce.2 = (f32[16,16]{1,0:T(8,128)S(1)}, f32[16,16]{1,0:T(8,128)S(1)}) all-reduce(f32[16,16]{1,0:T(8,128)S(1)} %fusion.54, f32[16,16]{1,0:T(8,128)S(1)} %fusion.53), channel_id=1, replica_groups=mesh['row'=16,'col'=32] {'row','col'}, use_global_device_ids=true, to_apply=%region_12.0 | all-reduce | flops 512 | bytes 4096 | tf_op jit(solution)/shard_map/psum | solution.py:27
  669.4 0.2 convolution_subtract_fusion.2
  669.6 0.2 convolution_subtract_fusion.1
  669.9 100.3 %psum.47 = f32[16,16]{0,1:T(8,128)S(1)} all-reduce(f32[16,16]{0,1:T(8,128)S(1)} %fusion.63), channel_id=1, replica_groups=mesh['row'=16,'col'=32] {'row','col'}, use_global_device_ids=true, to_apply=%region_14.0 | all-reduce | flops 256 | bytes 2048 | tf_op jit(solution)/shard_map/psum | solution.py:27
  770.3 1.5 cholesky.116
  771.8 0.7 compare_reduce_fusion
  772.5 0.7 select_bitcast_fusion
  773.3 2.0 dynamic-slice_select_fusion
  775.3 2.1 scatter.24
  777.4 0.8 scatter.25
  778.2 0.7 scatter.26
  779.0 0.2 fusion.64
  779.3 2.9 cholesky.41
  782.2 0.6 compare_reduce_fusion.3
  782.9 0.7 fusion.20
  783.5 2.4 custom-call.15
  786.0 0.2 fusion.47
  786.4 0.2 convolution_subtract_fusion
  786.6 0.1 fusion.37
  786.7 1.2 custom-call.22
  788.0 0.2 fusion.26
  788.4 0.2 convolution_add_fusion.3
  788.7 0.8 convolution_add_fusion.4
  789.5 0.8 convolution_add_fusion.2
  (68 shorter events, 3.4 us)
Async XLA Ops:
  7.2 0.7 copy-start
  7.2 139.5 %copy-start.3 = (f32[64]{0:T(128)S(1)}, f32[64]{0:T(128)}, u32[]{:S(2)}) copy-start(f32[64]{0:T(128)} %param.24) | copy-start | bytes 772
  7.2 139.5 %copy-start.2 = (f32[3,64]{1,0:T(4,128)S(1)}, f32[3,64]{1,0:T(4,128)}, u32[]{:S(2)}) copy-start(f32[3,64]{1,0:T(4,128)} %param.23) | copy-start | bytes 2308
  7.2 248.6 %reduce-scatter.7.cloned.1.call-start = ((), (), s32[]{:S(2)}) async-start(), calls=%async_computation.2 | async-start | bytes 557056
  194.9 61.7 %copy-start.1 = (f32[64]{0:T(128)S(1)}, f32[64]{0:T(128)}, u32[]{:S(2)}) copy-start(f32[64]{0:T(128)} %param.25) | copy-start | bytes 772
  195.9 360.5 %reduce-scatter.9.cloned.1.call-start = ((), (), s32[]{:S(2)}) async-start(), calls=%async_computation.3 | async-start | bytes 557056
  502.3 1.6 copy-start.4
Sparse Core Ops, SparseCore 0:
  196.0 59.6 reduce-scatter.6
  503.4 52.9 reduce-scatter.8
where the time goes:
time: 798 us; the launch traced here: 797 us
  blocking collectives  626 us (78%)
  waiting for transfers between devices  111 us (14%)
  other arithmetic  22.3 us (3%)
  between operations  14.2 us (2%)
  matrix products  13.4 us (2%)
  local copies, waits for them, and re-layouts  10.1 us (1%)
    psum x5, blocking collectives, reduce_small(): return lax.psum(terms, ('row', 'col'))  535 us
    unnamed x4, waiting for transfers between devices  111 us
    all_gather x2, blocking collectives, body(): lax.all_gather(field.astype(jnp.bfloat16), 'col', axis=1, tiled=True)  47.3 us
    all_gather x1, blocking collectives, body(): sources = lax.all_gather(geom, 'col', axis=1, tiled=True)  23.6 us
    all_gather x1, blocking collectives, body(): targets = lax.all_gather(centroids, 'row', axis=1, tiled=True)  19.9 us
  transfers between devices with their start and end apart: 2, of which 2 were waited for; matrix products, arithmetic and copies ran while one was open for 0% of the time, Pallas kernels for 0%

commit v1 on v0

--- a/solution.py
+++ b/solution.py
@@ -1,8 +1,17 @@
+import functools
 import math
 import jax
 import jax.numpy as jnp
 from jax import lax
 from jax.sharding import PartitionSpec as P
+
+
+def _list_pages(w_in, axis_tag, dev_axis):
+    taken_in = lax.psum(lax.psum(w_in, axis_name=axis_tag), axis_name=dev_axis)
+    return taken_in
+
+
+manage_rows_all = functools.partial(_list_pages, axis_tag="row", dev_axis="col")
 
 
 def kernel_tile(src, tgt, scale, delta2):
@@ -24,7 +33,7 @@
 
 
 def reduce_small(terms):
-    return lax.psum(terms, ("row", "col"))
+    return manage_rows_all(terms)
 
 
 def body(centroids, areas, conductance, power):

time: 798 us -> 838 us (1.050)
  blocking collectives: 626 us -> 666 us
    psum x5 -> x10, blocking collectives: 535 us -> 579 us  [_list_pages(): taken_in = lax.psum(lax.psum(w_in, axis_name=axis_tag), axis_name=dev_axis)]
where the time goes in v1:
time: 838 us
  blocking collectives  666 us (79%)
  waiting for transfers between devices  112 us (13%)
  other arithmetic  22.3 us (3%)
  between operations  14.3 us (2%)
  matrix products  13.4 us (2%)
  local copies, waits for them, and re-layouts  10.1 us (1%)
    psum x10, blocking collectives, _list_pages(): taken_in = lax.psum(lax.psum(w_in, axis_name=axis_tag), axis_name=dev_axis)  579 us
    unnamed x4, waiting for transfers between devices  112 us
    all_gather x2, blocking collectives, body(): lax.all_gather(field.astype(jnp.bfloat16), 'col', axis=1, tiled=True)  42.4 us
    all_gather x1, blocking collectives, body(): sources = lax.all_gather(geom, 'col', axis=1, tiled=True)  25.1 us
    all_gather x1, blocking collectives, body(): targets = lax.all_gather(centroids, 'row', axis=1, tiled=True)  19.1 us
  transfers between devices with their start and end apart: 2, of which 2 were waited for; matrix products, arithmetic and copies ran while one was open for 0% of the time, Pallas kernels for 0%

profile of v1, /device:TPU:1, one launch (start us, length us, event | category | flops | bytes accessed | tf_op | source)
XLA Modules:
  0.0 837.8 jit_solution(7439975555932855040)
XLA Ops:
  7.3 0.6 copy-done
  8.0 30.8 %psum.84 = f32[16,16]{0,1:T(8,128)S(1)} all-reduce(f32[16,16]{0,1:T(8,128)S(1)} %fusion.59), channel_id=1, replica_groups=mesh['row'=16,'col'=32] {'row'}, use_global_device_ids=true, to_apply=%region_0.0 | all-reduce | flops 256 | bytes 2048 | tf_op jit(solution)/shard_map/psum | solution.py:10
  38.8 71.0 %psum.85 = f32[16,16]{0,1:T(8,128)S(1)} all-reduce(f32[16,16]{0,1:T(8,128)S(1)} %psum.84), channel_id=1, replica_groups=mesh['row'=16,'col'=32] {'col'}, use_global_device_ids=true, to_apply=%region_1.0 | all-reduce | flops 256 | bytes 2048 | tf_op jit(solution)/shard_map/psum | solution.py:10
  109.9 1.5 cholesky.94
  111.4 0.6 compare_reduce_fusion.2
  112.0 0.6 fusion.49
  112.7 1.2 custom-call.20
  113.9 0.2 fusion.30
  114.2 21.0 %all-gather = bf16[32,64,16]{1,2,0:T(8,128)(2,1)S(1)} all-gather(bf16[1,64,16]{1,2,0:T(8,128)(2,1)S(1)} %convert_bitcast_fusion.1), channel_id=1, replica_groups=mesh['row'=16,'col'=32] {'col'}, dimensions={0}, use_global_device_ids=true | all-gather | bytes 67584 | tf_op jit(solution)/shard_map/all_gather | solution.py:57
  135.6 25.1 %all-gather.1 = f32[32,64,4]{1,2,0:T(4,128)S(1)} all-gather(f32[1,64,4]{1,2,0:T(4,128)S(1)} %maximum_bitcast_fusion), channel_id=1, replica_groups=mesh['row'=16,'col'=32] {'col'}, dimensions={0}, use_global_device_ids=true | all-gather | bytes 33792 | tf_op jit(solution)/shard_map/all_gather | solution.py:47
  160.7 19.1 %all-gather.2 = f32[16,64,3]{1,2,0:T(4,128)S(1)} all-gather(f32[1,64,3]{1,2,0:T(4,128)S(1)} %bitcast.175), channel_id=1, replica_groups=mesh['row'=16,'col'=32] {'row'}, dimensions={0}, use_global_device_ids=true | all-gather | bytes 13056 | tf_op jit(solution)/shard_map/all_gather | solution.py:48
  179.9 4.5 while.34
  180.0 1.0 convolution_add_fusion.7
  181.2 1.0 convolution_add_fusion.7
  182.3 1.0 convolution_add_fusion.7
  183.4 1.0 convolution_add_fusion.7
  184.4 1.0 copy.57
  185.5 58.7 %reduce-scatter.7.cloned.1.call-done = f32[64,16]{1,0:T(8,128)} async-done(((f32[1024,16]{1,0:T(8,128)}), f32[64,16]{1,0:T(8,128)}) %reduce-scatter.7.cloned.1.call-update) | async-done | bytes 4112
  244.2 0.8 copy.58
  245.2 22.5 %psum.86 = f32[16,16]{1,0:T(8,128)S(1)} all-reduce(f32[16,16]{1,0:T(8,128)S(1)} %fusion.46), channel_id=1, replica_groups=mesh['row'=16,'col'=32] {'row'}, use_global_device_ids=true, to_apply=%region_7.0 | all-reduce | flops 256 | bytes 2048 | tf_op jit(solution)/shard_map/psum | solution.py:10
  267.7 81.1 %psum.87 = f32[16,16]{1,0:T(8,128)S(1)} all-reduce(f32[16,16]{1,0:T(8,128)S(1)} %psum.86), channel_id=1, replica_groups=mesh['row'=16,'col'=32] {'col'}, use_global_device_ids=true, to_apply=%region_8.0 | all-reduce | flops 256 | bytes 2048 | tf_op jit(solution)/shard_map/psum | solution.py:10
  348.8 0.2 convolution_subtract_fusion.3
  349.2 22.2 %psum.88 = f32[16,16]{0,1:T(8,128)S(1)} all-reduce(f32[16,16]{0,1:T(8,128)S(1)} %fusion.61), channel_id=1, replica_groups=mesh['row'=16,'col'=32] {'row'}, use_global_device_ids=true, to_apply=%region_9.0 | all-reduce | flops 256 | bytes 2048 | tf_op jit(solution)/shard_map/psum | solution.py:10
  371.4 70.8 %psum.89 = f32[16,16]{0,1:T(8,128)S(1)} all-reduce(f32[16,16]{0,1:T(8,128)S(1)} %psum.88), channel_id=1, replica_groups=mesh['row'=16,'col'=32] {'col'}, use_global_device_ids=true, to_apply=%region_10.0 | all-reduce | flops 256 | bytes 2048 | tf_op jit(solution)/shard_map/psum | solution.py:10
  442.3 1.5 cholesky.105
  443.7 0.6 compare_reduce_fusion.1
  444.4 0.6 select_bitcast_fusion.1
  445.0 1.2 custom-call.21
  446.3 0.2 fusion.28
  446.6 21.3 %all-gather.3 = bf16[32,64,16]{1,2,0:T(8,128)(2,1)S(1)} all-gather(bf16[1,64,16]{1,2,0:T(8,128)(2,1)S(1)} %convert_bitcast_fusion), channel_id=1, replica_groups=mesh['row'=16,'col'=32] {'col'}, dimensions={0}, use_global_device_ids=true | all-gather | bytes 67584 | tf_op jit(solution)/shard_map/all_gather | solution.py:57
  468.2 4.5 while.35
  468.3 1.0 convolution_add_fusion.8
  469.4 1.0 convolution_add_fusion.8
  470.5 1.0 convolution_add_fusion.8
  471.7 1.0 convolution_add_fusion.8
  472.7 1.0 copy.59
  473.7 0.6 fusion.58
  474.3 0.7 and_reduce_fusion
  475.1 0.5 scatter.21
  475.6 52.9 %reduce-scatter.9.cloned.1.call-done = f32[64,16]{1,0:T(8,128)} async-done(((f32[1024,16]{1,0:T(8,128)}), f32[64,16]{1,0:T(8,128)}) %reduce-scatter.9.cloned.1.call-update) | async-done | bytes 4112
  528.5 0.8 copy.60
  529.5 40.7 %all-reduce.3 = (f32[16,16]{1,0:T(8,128)S(1)}, f32[16,16]{1,0:T(8,128)S(1)}) all-reduce(f32[16,16]{1,0:T(8,128)S(1)} %fusion.54, f32[16,16]{1,0:T(8,128)S(1)} %fusion.53), channel_id=1, replica_groups=mesh['row'=16,'col'=32] {'row'}, use_global_device_ids=true, to_apply=%region_15.0 | all-reduce | flops 512 | bytes 4096 | tf_op jit(solution)/shard_map/psum | solution.py:10
  570.2 143.3 %all-reduce.2 = (f32[16,16]{1,0:T(8,128)S(1)}, f32[16,16]{1,0:T(8,128)S(1)}) all-reduce(f32[16,16]{1,0:T(8,128)S(1)} %get-tuple-element.324, f32[16,16]{1,0:T(8,128)S(1)} %get-tuple-element.325), channel_id=1, replica_groups=mesh['row'=16,'col'=32] {'col'}, use_global_device_ids=true, to_apply=%region_16.0 | all-reduce | flops 512 | bytes 4096 | tf_op jit(solution)/shard_map/psum | solution.py:10
  713.5 0.2 convolution_subtract_fusion.2
  713.7 0.2 convolution_subtract_fusion.1
  714.0 21.2 %psum.94 = f32[16,16]{0,1:T(8,128)S(1)} all-reduce(f32[16,16]{0,1:T(8,128)S(1)} %fusion.63), channel_id=1, replica_groups=mesh['row'=16,'col'=32] {'row'}, use_global_device_ids=true, to_apply=%region_19.0 | all-reduce | flops 256 | bytes 2048 | tf_op jit(solution)/shard_map/psum | solution.py:10
  735.2 75.7 %psum.95 = f32[16,16]{0,1:T(8,128)S(1)} all-reduce(f32[16,16]{0,1:T(8,128)S(1)} %psum.94), channel_id=1, replica_groups=mesh['row'=16,'col'=32] {'col'}, use_global_device_ids=true, to_apply=%region_20.0 | all-reduce | flops 256 | bytes 2048 | tf_op jit(solution)/shard_map/psum | solution.py:10
  811.0 1.5 cholesky.116
  812.5 0.7 compare_reduce_fusion
  813.2 0.7 select_bitcast_fusion
  814.0 2.0 dynamic-slice_select_fusion
  816.0 2.1 scatter.24
  818.1 0.8 scatter.25
  818.9 0.7 scatter.26
  819.7 0.2 fusion.64
  820.0 2.9 cholesky.41
  822.9 0.6 compare_reduce_fusion.3
  823.6 0.7 fusion.20
  824.2 2.4 custom-call.15
  827.4 1.2 custom-call.22
  828.7 0.2 fusion.26
  829.1 0.2 convolution_add_fusion.3
  829.3 0.8 convolution_add_fusion.4
  830.2 0.8 convolution_add_fusion.2
  (73 shorter events, 4.2 us)
Async XLA Ops:
  7.2 0.7 copy-start
  7.2 128.3 %copy-start.3 = (f32[64]{0:T(128)S(1)}, f32[64]{0:T(128)}, u32[]{:S(2)}) copy-start(f32[64]{0:T(128)} %param.24) | copy-start | bytes 772
  7.2 128.3 %copy-start.2 = (f32[3,64]{1,0:T(4,128)S(1)}, f32[3,64]{1,0:T(4,128)}, u32[]{:S(2)}) copy-start(f32[3,64]{1,0:T(4,128)} %param.23) | copy-start | bytes 2308
  7.2 237.0 %reduce-scatter.7.cloned.1.call-start = ((), (), s32[]{:S(2)}) async-start(), calls=%async_computation.2 | async-start | bytes 557056
  184.4 60.6 %copy-start.1 = (f32[64]{0:T(128)S(1)}, f32[64]{0:T(128)}, u32[]{:S(2)}) copy-start(f32[64]{0:T(128)} %param.25) | copy-start | bytes 772
  185.4 343.0 %reduce-scatter.9.cloned.1.call-start = ((), (), s32[]{:S(2)}) async-start(), calls=%async_computation.3 | async-start | bytes 557056
  472.7 1.6 copy-start.4
Sparse Core Ops, SparseCore 0:
  185.6 58.5 reduce-scatter.6
  473.8 54.6 reduce-scatter.8
